TPU v7x, 32 devices: a whole 2x2x4 slice. The times are simulated.
32 devices in a mesh: groups: 2 (over y), ctx: 8 (over z, x), tp: 2 (over core).
Axes of the slice: x: 2, y: 2, z: 4, core: 2. Of those that a mesh axis runs over, the one named last changes fastest.
Arguments:
- normed_input: bfloat16 [4096, 2688], P(('groups', 'ctx')), parts along dimension 0, may hold values from -6 to 6
- attn_queries: bfloat16 [4096, 2048], P(('groups', 'ctx'), 'tp'), parts along dimension 0, may hold values from -45 to 45
- attn_keys: bfloat16 [4096, 1024], P(('groups', 'ctx'), 'tp'), parts along dimension 0, may hold values from -9 to 9
- attn_values: bfloat16 [4096, 1024], P(('groups', 'ctx'), 'tp'), parts along dimension 0, may hold values from -6 to 6
- out_grad: bfloat16 [4096, 2048], P(('groups', 'ctx'), 'tp'), parts along dimension 0, may hold values from -6 to 6
Outputs:
- query_grad: bfloat16 [4096, 2048], P(('groups', 'ctx'), 'tp'), parts along dimension 0
- key_weight_grad: float32 [5376, 1024], P(('groups', 'ctx'), 'tp'), parts along dimension 0
- value_grad: bfloat16 [4096, 1024], P(('groups', 'ctx'), 'tp'), parts along dimension 0
There are 2 independent parts, one for each index of `groups`. A program takes and returns all parts, laid end to end along the dimension named above; each array names one. Nothing has to cross between parts.
All inputs are finite; a program needn't handle non-finite values.
Results may differ from a plain program's by a relative error of at most 0.0053.
Values may be sent and summed in bfloat16 or wider, within the bound.
A program may use at most 128 MiB of HBM per device.

v0:
```python
import jax
import jax.numpy as jnp
from jax import lax
from jax.sharding import PartitionSpec as P

HD = 128
HQ = 16
HK = 8
W = 1024


attn_scale = 168.0 ** (-0.5)


def shifted(value, axis, steps):
    count = lax.axis_size(axis)
    first, last = (max(0, -steps), min(count, count - steps))
    return lax.ppermute(value, axis, [(source, source + steps) for source in range(first, last)])


def head_block(query_head, grad_head, key_head, value_head, allowed):
    scores = attn_scale * jnp.einsum(
        "qgd,kd->gqk", query_head, key_head, preferred_element_type=jnp.float32
    )
    scores = jnp.where(allowed, scores, -jnp.inf)
    row_max = jnp.max(scores, axis=-1, keepdims=True)
    raised = jnp.exp(scores - row_max)
    soft_weights = raised / jnp.sum(raised, axis=-1, keepdims=True)
    soft_low = soft_weights.astype(jnp.bfloat16)
    grad_probs = jnp.einsum(
        "qgd,kd->gqk", grad_head, value_head, preferred_element_type=jnp.float32
    )
    row_delta = jnp.sum(soft_weights * grad_probs, axis=-1, keepdims=True)
    grad_scores = (soft_weights * (grad_probs - row_delta)).astype(jnp.bfloat16)
    grad_query = attn_scale * jnp.einsum(
        "gqk,kd->qgd", grad_scores, key_head, preferred_element_type=jnp.float32
    )
    grad_key = attn_scale * jnp.einsum(
        "gqk,qgd->kd", grad_scores, query_head, preferred_element_type=jnp.float32
    )
    grad_value = jnp.einsum("gqk,qgd->kd", soft_low, grad_head, preferred_element_type=jnp.float32)
    return (grad_query.astype(jnp.bfloat16), grad_key, grad_value)


def shards(normed_input, attn_queries, attn_keys, attn_values, out_grad):
    tokens_here = attn_queries.shape[0]
    kv_width = attn_keys.shape[1]
    heads_here = kv_width // HD
    group_size = HQ // HK
    reach_count = max(1, W // tokens_here)
    edge_rows = min(W, tokens_here)
    block_rows = min(512, tokens_here)
    window_rows = block_rows + W
    halo_keys = []
    halo_values = []
    for distance in range(reach_count, 0, -1):
        far_keys, far_values = shifted((attn_keys, attn_values), "ctx", distance)
        halo_keys.append(far_keys)
        halo_values.append(far_values)
    every_key = jnp.concatenate(halo_keys + [attn_keys], axis=0)
    every_value = jnp.concatenate(halo_values + [attn_values], axis=0)
    first_row = lax.axis_index("ctx") * tokens_here
    query_offsets = jnp.arange(block_rows, dtype=jnp.int32)
    key_offsets = jnp.arange(window_rows, dtype=jnp.int32)
    key_grads = [jnp.zeros((W + tokens_here, HD), jnp.float32) for head_index in range(heads_here)]
    value_grads = [
        jnp.zeros((W + tokens_here, HD), jnp.float32) for head_index in range(heads_here)
    ]
    query_pos = first_row + 0 + query_offsets
    key_pos = first_row + 0 - W + key_offsets
    distance_back = query_pos[:, None] - key_pos[None, :]
    allowed = (distance_back >= 0) & (distance_back < W) & (key_pos[None, :] >= 0)
    columns = []
    for head_index in range(heads_here):
        query_cols = slice(head_index * group_size * HD, (head_index + 1) * group_size * HD)
        kv_cols = slice(head_index * HD, (head_index + 1) * HD)
        query_head = attn_queries[0:block_rows, query_cols].reshape(block_rows, group_size, HD)
        grad_head = out_grad[0:block_rows, query_cols].reshape(block_rows, group_size, HD)
        key_head = every_key[0:window_rows, kv_cols]
        value_head = every_value[0:window_rows, kv_cols]
        grad_query, grad_key, grad_value = head_block(
            query_head, grad_head, key_head, value_head, allowed
        )
        columns.append(grad_query.reshape(block_rows, group_size * HD))
        key_grads[head_index] = key_grads[head_index].at[0:window_rows].add(grad_key)
        value_grads[head_index] = value_grads[head_index].at[0:window_rows].add(grad_value)
    query_rows = jnp.concatenate(columns, axis=1)
    key_total = jnp.concatenate(key_grads, axis=1)
    value_total = jnp.concatenate(value_grads, axis=1)
    own_keys = key_total[W:]
    own_values = value_total[W:]
    for distance in range(1, reach_count + 1):
        slot_index = reach_count - distance
        back_keys, back_values = shifted(
            (
                key_total[slot_index * edge_rows : (slot_index + 1) * edge_rows],
                value_total[slot_index * edge_rows : (slot_index + 1) * edge_rows],
            ),
            "ctx",
            -distance,
        )
        own_keys = own_keys.at[tokens_here - edge_rows :].add(back_keys)
        own_values = own_values.at[tokens_here - edge_rows :].add(back_values)
    key_low = own_keys.astype(jnp.bfloat16)
    value_low = own_values.astype(jnp.bfloat16)
    contract = (((0,), (0,)), ((), ()))
    partial_term = lax.dot_general(
        normed_input, key_low, contract, preferred_element_type=jnp.float32
    )
    summed = lax.psum_scatter(partial_term, "ctx", scatter_dimension=0, tiled=True)
    return (query_rows, summed, value_low)


def solution(mesh):
    return jax.shard_map(
        shards,
        mesh=mesh,
        in_specs=(
            P(("groups", "ctx"), None),
            P(("groups", "ctx"), "tp"),
            P(("groups", "ctx"), "tp"),
            P(("groups", "ctx"), "tp"),
            P(("groups", "ctx"), "tp"),
        ),
        out_specs=(
            P(("groups", "ctx"), "tp"),
            P(("groups", "ctx"), "tp"),
            P(("groups", "ctx"), "tp"),
        ),
        check_vma=False,
    )
```

profile of v0, /device:TPU:0, one launch (start us, length us, event | category | flops | bytes accessed | tf_op | source)
XLA Modules:
  0.0 362.8 jit_solution(14561726327072352522)
XLA Ops:
  7.2 5.8 %collective-permute-start.2 = (bf16[256,512]{1,0:T(8,128)(2,1)}, bf16[256,512]{1,0:T(8,128)(2,1)}, u32[]{:S(2)}, u32[]{:S(2)}) collective-permute-start(bf16[256,512]{1,0:T(8,128)(2,1)} %param.71), channel_id=1, source_target_pairs={{0,4},{2,6},{4,8},{6,10},{8,12},{10,14},{1,5},{3,7},{5,9},{7,11},{... | collective-permute-start | bytes 786440 | tf_op jit(solution)/shard_map/ppermute | solution.py:18
  13.0 4.4 %collective-permute-start.1 = (bf16[256,512]{1,0:T(8,128)(2,1)}, bf16[256,512]{1,0:T(8,128)(2,1)}, u32[]{:S(2)}, u32[]{:S(2)}) collective-permute-start(bf16[256,512]{1,0:T(8,128)(2,1)} %param.71), channel_id=1, source_target_pairs={{0,6},{2,8},{4,10},{6,12},{8,14},{1,7},{3,9},{5,11},{7,13},{9,15},... | collective-permute-start | bytes 786440 | tf_op jit(solution)/shard_map/ppermute | solution.py:18
  17.4 3.5 collective-permute-start.6
  22.2 2.0 collective-permute-start.4
  24.3 1.6 fusion.29
  33.0 7.7 %collective-permute-done.4 = bf16[256,512]{1,0:T(8,128)(2,1)} collective-permute-done((bf16[256,512]{1,0:T(8,128)(2,1)}, bf16[256,512]{1,0:T(8,128)(2,1)}, u32[]{:S(2)}, u32[]{:S(2)}) %collective-permute-start.4) | collective-permute-done | bytes 262176 | tf_op jit(solution)/shard_map/ppermute | solution.py:18
  40.7 3.4 collective-permute-start.7
  45.1 5.3 %collective-permute-start = (bf16[256,512]{1,0:T(8,128)(2,1)}, bf16[256,512]{1,0:T(8,128)(2,1)S(1)}, u32[]{:S(2)}, u32[]{:S(2)}) collective-permute-start(bf16[256,512]{1,0:T(8,128)(2,1)} %param.71), channel_id=1, source_target_pairs={{0,8},{2,10},{4,12},{6,14},{1,9},{3,11},{5,13},{7,15},{16,24},{18,... | collective-permute-start | bytes 786440 | tf_op jit(solution)/shard_map/ppermute | solution.py:18
  50.5 8.9 %collective-permute-start.3 = (bf16[256,512]{1,0:T(8,128)(2,1)}, bf16[256,512]{1,0:T(8,128)(2,1)S(1)}, u32[]{:S(2)}, u32[]{:S(2)}) collective-permute-start(bf16[256,512]{1,0:T(8,128)(2,1)} %param.71), channel_id=1, source_target_pairs={{0,2},{2,4},{4,6},{6,8},{8,10},{10,12},{12,14},{1,3},{3,5},{5,7},{... | collective-permute-start | bytes 786440 | tf_op jit(solution)/shard_map/ppermute | solution.py:18
  61.8 2.1 collective-permute-done.3
  64.9 2.4 fusion.62
  67.3 2.5 multiply_reduce_fusion.3
  71.4 3.6 fusion.61
  75.0 2.6 multiply_reduce_fusion.2
  80.6 3.5 fusion.60
  84.1 2.6 multiply_reduce_fusion.1
  89.7 3.6 fusion.59
  93.3 2.6 multiply_reduce_fusion
  103.7 35.4 %collective-permute-done.8 = f32[256,512]{0,1:T(8,128)S(1)} collective-permute-done((f32[256,512]{0,1:T(8,128)S(1)}, f32[256,512]{0,1:T(8,128)S(1)}, u32[]{:S(2)}, u32[]{:S(2)}) %collective-permute-start.8) | collective-permute-done | bytes 524320 | tf_op jit(solution)/shard_map/ppermute | solution.py:18
  139.1 29.5 %collective-permute-done.11 = f32[256,512]{0,1:T(8,128)S(1)} collective-permute-done((f32[256,512]{0,1:T(8,128)S(1)}, f32[256,512]{0,1:T(8,128)S(1)}, u32[]{:S(2)}, u32[]{:S(2)}) %collective-permute-start.11) | collective-permute-done | bytes 524320 | tf_op jit(solution)/shard_map/ppermute | solution.py:18
  168.7 3.5 convolution_bitcast_fusion
  172.2 6.2 %copy.142 = f32[2688,512]{1,0:T(8,128)} copy(f32[2688,512]{0,1:T(8,128)} %convolution_bitcast_fusion) | data formatting | bytes 11010048
  179.3 2.6 convolution_bitcast_fusion.8
  181.9 2.6 convolution_bitcast_fusion.7
  184.5 2.6 convolution_bitcast_fusion.6
  187.1 3.5 convolution_bitcast_fusion.5
  193.3 1.5 collective-permute-start.12
  200.2 1.9 fusion.33
  203.1 20.5 %collective-permute-done.12 = f32[256,512]{0,1:T(8,128)S(1)} collective-permute-done((f32[256,512]{0,1:T(8,128)}, f32[256,512]{0,1:T(8,128)S(1)}, u32[]{:S(2)}, u32[]{:S(2)}) %collective-permute-start.12) | collective-permute-done | bytes 524320 | tf_op jit(solution)/shard_map/ppermute | solution.py:18
  223.6 72.1 %collective-permute-done.15 = f32[256,512]{0,1:T(8,128)} collective-permute-done((f32[256,512]{0,1:T(8,128)}, f32[256,512]{0,1:T(8,128)}, u32[]{:S(2)}, u32[]{:S(2)}) %collective-permute-start.15) | collective-permute-done | bytes 524320 | tf_op jit(solution)/shard_map/ppermute | solution.py:18
  295.7 1.7 fusion.37
  298.2 57.8 %reduce-scatter.4.cloned.1.call-done = f32[336,512]{1,0:T(8,128)} async-done(((f32[2688,512]{1,0:T(8,128)}), f32[336,512]{1,0:T(8,128)}) %reduce-scatter.4.cloned.1.call-update) | async-done | bytes 688144
  (120 shorter events, 38.8 us)
Async XLA Ops:
  7.2 161.5 %copy-start = (bf16[256,2688]{1,0:T(8,128)(2,1)S(1)}, bf16[256,2688]{1,0:T(8,128)(2,1)}, u32[]{:S(2)}) copy-start(bf16[256,2688]{1,0:T(8,128)(2,1)} %param.69) | copy-start | bytes 4128772
  7.2 33.5 %copy-start.23 = (bf16[256,512]{1,0:T(8,128)(2,1)S(1)}, bf16[256,512]{1,0:T(8,128)(2,1)}, u32[]{:S(2)}) copy-start(bf16[256,512]{1,0:T(8,128)(2,1)} %param.72) | copy-start | bytes 786436
  7.2 348.8 %reduce-scatter.4.cloned.1.call-start = ((), (), s32[]{:S(2)}) async-start(), calls=%async_computation.1 | async-start | bytes 6193152
  7.2 53.5 %collective-permute-start.2 = (bf16[256,512]{1,0:T(8,128)(2,1)}, bf16[256,512]{1,0:T(8,128)(2,1)}, u32[]{:S(2)}, u32[]{:S(2)}) collective-permute-start(bf16[256,512]{1,0:T(8,128)(2,1)} %param.71), channel_id=1, source_target_pairs={{0,4},{2,6},{4,8},{6,10},{8,12},{10,14},{1,5},{3,7},{5,9},{7,11},{... | collective-permute-start | bytes 786440 | tf_op jit(solution)/shard_map/ppermute | solution.py:18
  13.0 46.6 %collective-permute-start.1 = (bf16[256,512]{1,0:T(8,128)(2,1)}, bf16[256,512]{1,0:T(8,128)(2,1)}, u32[]{:S(2)}, u32[]{:S(2)}) collective-permute-start(bf16[256,512]{1,0:T(8,128)(2,1)} %param.71), channel_id=1, source_target_pairs={{0,6},{2,8},{4,10},{6,12},{8,14},{1,7},{3,9},{5,11},{7,13},{9,15},... | collective-permute-start | bytes 786440 | tf_op jit(solution)/shard_map/ppermute | solution.py:18
  17.4 33.1 %collective-permute-start.6 = (bf16[256,512]{1,0:T(8,128)(2,1)}, bf16[256,512]{1,0:T(8,128)(2,1)S(1)}, u32[]{:S(2)}, u32[]{:S(2)}) collective-permute-start(bf16[256,512]{1,0:T(8,128)(2,1)} %param.72), channel_id=1, source_target_pairs={{0,4},{2,6},{4,8},{6,10},{8,12},{10,14},{1,5},{3,7},{5,9},{7,11},{... | collective-permute-start | bytes 786440 | tf_op jit(solution)/shard_map/ppermute | solution.py:18
  20.9 24.2 %collective-permute-start.5 = (bf16[256,512]{1,0:T(8,128)(2,1)}, bf16[256,512]{1,0:T(8,128)(2,1)S(1)}, u32[]{:S(2)}, u32[]{:S(2)}) collective-permute-start(bf16[256,512]{1,0:T(8,128)(2,1)} %param.72), channel_id=1, source_target_pairs={{0,6},{2,8},{4,10},{6,12},{8,14},{1,7},{3,9},{5,11},{7,13},{9,15},... | collective-permute-start | bytes 786440 | tf_op jit(solution)/shard_map/ppermute | solution.py:18
  22.2 18.4 %collective-permute-start.4 = (bf16[256,512]{1,0:T(8,128)(2,1)}, bf16[256,512]{1,0:T(8,128)(2,1)}, u32[]{:S(2)}, u32[]{:S(2)}) collective-permute-start(bf16[256,512]{1,0:T(8,128)(2,1)} %param.72), channel_id=1, source_target_pairs={{0,8},{2,10},{4,12},{6,14},{1,9},{3,11},{5,13},{7,15},{16,24},{18,... | collective-permute-start | bytes 786440 | tf_op jit(solution)/shard_map/ppermute | solution.py:18
  28.3 36.6 %copy-start.17 = (bf16[256,256]{0,1:T(8,128)(2,1)}, bf16[256,256]{0,1:T(8,128)(2,1)S(1)}, u32[]{:S(2)}) copy-start(bf16[256,256]{0,1:T(8,128)(2,1)S(1)} %copy.144) | copy-start | bytes 393220
  33.0 32.0 %copy-start.22 = (pred[256,1280]{0,1:T(8,128)(4,1)S(1)}, pred[256,1280]{0,1:T(8,128)(4,1)}, u32[]{:S(2)}) copy-start(pred[256,1280]{0,1:T(8,128)(4,1)} %fusion.29) | copy-start | bytes 983044
  40.7 18.8 %collective-permute-start.7 = (bf16[256,512]{1,0:T(8,128)(2,1)S(1)}, bf16[256,512]{1,0:T(8,128)(2,1)S(1)}, u32[]{:S(2)}, u32[]{:S(2)}) collective-permute-start(bf16[256,512]{1,0:T(8,128)(2,1)S(1)} %copy-done.23), channel_id=1, source_target_pairs={{0,2},{2,4},{4,6},{6,8},{8,10},{10,12},{12,14},{1,3},{3,5},{5,7},{... | collective-permute-start | bytes 786440 | tf_op jit(solution)/shard_map/ppermute | solution.py:18
  45.1 14.4 %collective-permute-start = (bf16[256,512]{1,0:T(8,128)(2,1)}, bf16[256,512]{1,0:T(8,128)(2,1)S(1)}, u32[]{:S(2)}, u32[]{:S(2)}) collective-permute-start(bf16[256,512]{1,0:T(8,128)(2,1)} %param.71), channel_id=1, source_target_pairs={{0,8},{2,10},{4,12},{6,14},{1,9},{3,11},{5,13},{7,15},{16,24},{18,... | collective-permute-start | bytes 786440 | tf_op jit(solution)/shard_map/ppermute | solution.py:18
  50.5 13.4 %collective-permute-start.3 = (bf16[256,512]{1,0:T(8,128)(2,1)}, bf16[256,512]{1,0:T(8,128)(2,1)S(1)}, u32[]{:S(2)}, u32[]{:S(2)}) collective-permute-start(bf16[256,512]{1,0:T(8,128)(2,1)} %param.71), channel_id=1, source_target_pairs={{0,2},{2,4},{4,6},{6,8},{8,10},{10,12},{12,14},{1,3},{3,5},{5,7},{... | collective-permute-start | bytes 786440 | tf_op jit(solution)/shard_map/ppermute | solution.py:18
  59.6 5.3 %copy-start.27 = (bf16[1280,512]{1,0:T(8,128)(2,1)}, bf16[1280,512]{1,0:T(8,128)(2,1)S(1)}, u32[]{:S(2)}) copy-start(bf16[1280,512]{1,0:T(8,128)(2,1)S(1)} %constant_dynamic-update-slice_fusion.5) | copy-start | bytes 3932164
  67.3 2.6 copy-start.11
  75.0 2.7 copy-start.12
  84.1 2.7 copy-start.13
  93.3 2.7 copy-start.10
  98.4 40.8 %collective-permute-start.8 = (f32[256,512]{0,1:T(8,128)S(1)}, f32[256,512]{0,1:T(8,128)S(1)}, u32[]{:S(2)}, u32[]{:S(2)}) collective-permute-start(f32[256,512]{0,1:T(8,128)S(1)} %get-tuple-element.336), channel_id=1, source_target_pairs={{2,0},{4,2},{6,4},{8,6},{10,8},{12,10},{14,12},{3,1},{5,3},{7,5},{... | collective-permute-start | bytes 1572872 | tf_op jit(solution)/shard_map/ppermute | solution.py:18
  99.7 69.0 %collective-permute-start.11 = (f32[256,512]{0,1:T(8,128)S(1)}, f32[256,512]{0,1:T(8,128)S(1)}, u32[]{:S(2)}, u32[]{:S(2)}) collective-permute-start(f32[256,512]{0,1:T(8,128)S(1)} %get-tuple-element.337), channel_id=1, source_target_pairs={{8,0},{10,2},{12,4},{14,6},{9,1},{11,3},{13,5},{15,7},{24,16},{26,... | collective-permute-start | bytes 1572872 | tf_op jit(solution)/shard_map/ppermute | solution.py:18
  101.0 67.7 %collective-permute-start.10 = (f32[256,512]{0,1:T(8,128)S(1)}, f32[256,512]{0,1:T(8,128)S(1)}, u32[]{:S(2)}, u32[]{:S(2)}) collective-permute-start(f32[256,512]{0,1:T(8,128)S(1)} %get-tuple-element.338), channel_id=1, source_target_pairs={{6,0},{8,2},{10,4},{12,6},{14,8},{7,1},{9,3},{11,5},{13,7},{15,9},... | collective-permute-start | bytes 1572872 | tf_op jit(solution)/shard_map/ppermute | solution.py:18
  102.3 66.4 %collective-permute-start.9 = (f32[256,512]{0,1:T(8,128)S(1)}, f32[256,512]{0,1:T(8,128)S(1)}, u32[]{:S(2)}, u32[]{:S(2)}) collective-permute-start(f32[256,512]{0,1:T(8,128)S(1)} %get-tuple-element.339), channel_id=1, source_target_pairs={{4,0},{6,2},{8,4},{10,6},{12,8},{14,10},{5,1},{7,3},{9,5},{11,7},{... | collective-permute-start | bytes 1572872 | tf_op jit(solution)/shard_map/ppermute | solution.py:18
  179.3 2.6 copy-start.26
  191.9 7.2 %copy-start.7 = (f32[1280,512]{0,1:T(8,128)}, f32[1280,512]{0,1:T(8,128)S(1)}, u32[]{:S(2)}) copy-start(f32[1280,512]{0,1:T(8,128)S(1)} %pad_maximum_fusion.1) | copy-start | bytes 7864324
  191.9 6.8 %copy-start.15 = (bf16[1280,512]{1,0:T(8,128)(2,1)S(1)}, bf16[1280,512]{1,0:T(8,128)(2,1)}, u32[]{:S(2)}) copy-start(bf16[1280,512]{1,0:T(8,128)(2,1)} %copy-done.14) | copy-start | bytes 3932164
  191.9 7.2 %copy-start.3 = (bf16[2,256,1280]{1,2,0:T(8,128)(2,1)S(1)}, bf16[2,256,1280]{1,2,0:T(8,128)(2,1)}, u32[]{:S(2)}) copy-start(bf16[2,256,1280]{1,2,0:T(8,128)(2,1)} %copy-done.2) | copy-start | bytes 3932164
  193.3 6.2 %copy-start.5 = (bf16[2,256,1280]{1,2,0:T(8,128)(2,1)S(1)}, bf16[2,256,1280]{1,2,0:T(8,128)(2,1)}, u32[]{:S(2)}) copy-start(bf16[2,256,1280]{1,2,0:T(8,128)(2,1)} %copy-done.4) | copy-start | bytes 3932164
  193.3 30.3 %collective-permute-start.12 = (f32[256,512]{0,1:T(8,128)}, f32[256,512]{0,1:T(8,128)S(1)}, u32[]{:S(2)}, u32[]{:S(2)}) collective-permute-start(f32[256,512]{0,1:T(8,128)} %get-tuple-element.332), channel_id=1, source_target_pairs={{2,0},{4,2},{6,4},{8,6},{10,8},{12,10},{14,12},{3,1},{5,3},{7,5},{... | collective-permute-start | bytes 1572872 | tf_op jit(solution)/shard_map/ppermute | solution.py:18
  194.8 100.8 %collective-permute-start.15 = (f32[256,512]{0,1:T(8,128)}, f32[256,512]{0,1:T(8,128)}, u32[]{:S(2)}, u32[]{:S(2)}) collective-permute-start(f32[256,512]{0,1:T(8,128)} %get-tuple-element.333), channel_id=1, source_target_pairs={{8,0},{10,2},{12,4},{14,6},{9,1},{11,3},{13,5},{15,7},{24,16},{26,... | collective-permute-start | bytes 1572872 | tf_op jit(solution)/shard_map/ppermute | solution.py:18
  196.1 99.5 %collective-permute-start.14 = (f32[256,512]{0,1:T(8,128)}, f32[256,512]{0,1:T(8,128)}, u32[]{:S(2)}, u32[]{:S(2)}) collective-permute-start(f32[256,512]{0,1:T(8,128)} %get-tuple-element.334), channel_id=1, source_target_pairs={{6,0},{8,2},{10,4},{12,6},{14,8},{7,1},{9,3},{11,5},{13,7},{15,9},... | collective-permute-start | bytes 1572872 | tf_op jit(solution)/shard_map/ppermute | solution.py:18
  197.4 98.2 %collective-permute-start.13 = (f32[256,512]{0,1:T(8,128)}, f32[256,512]{0,1:T(8,128)}, u32[]{:S(2)}, u32[]{:S(2)}) collective-permute-start(f32[256,512]{0,1:T(8,128)} %get-tuple-element.335), channel_id=1, source_target_pairs={{4,0},{6,2},{8,4},{10,6},{12,8},{14,10},{5,1},{7,3},{9,5},{11,7},{... | collective-permute-start | bytes 1572872 | tf_op jit(solution)/shard_map/ppermute | solution.py:18
  200.2 155.8 %copy-start.1 = (bf16[256,2688]{1,0:T(8,128)(2,1)S(1)}, bf16[256,2688]{1,0:T(8,128)(2,1)}, u32[]{:S(2)}) copy-start(bf16[256,2688]{1,0:T(8,128)(2,1)} %param.69) | copy-start | bytes 4128772
  (13 other events, 20.7 us)
Sparse Core Ops, SparseCore 0:
  178.5 177.4 reduce-scatter.3
where the time goes:
time: 364 us; the launch traced here: 363 us
  waiting for transfers between devices  225 us (62%)
  starting transfers between devices  45.5 us (12%)
  matrix products  44.8 us (12%)
  local copies, waits for them, and re-layouts  25.4 us (7%)
  between operations  14.6 us (4%)
  other arithmetic  7.22 us (2%)
    ppermute x16, waiting for transfers between devices, shifted(): lax.ppermute(value, axis, [(source, source + steps) for source in range(f...  167 us
    unnamed x2, waiting for transfers between devices  57.8 us
    ppermute x16, starting transfers between devices, shifted(): lax.ppermute(value, axis, [(source, source + steps) for source in range(f...  45.5 us
    unnamed x74, local copies, waits for them, and re-layouts  20.3 us
    sub x4, matrix products, head_block(): raised = jnp.exp(scores - row_max)  13 us
    dot_general x4, matrix products, head_block(): jnp.einsum('gqk,qgd->kd', soft_low, grad_head, preferred_element_type=jnp...  11.3 us
    dot_general x4, matrix products, head_block(): jnp.einsum('qgd,kd->gqk', grad_head, value_head, preferred_element_type=j...  10.2 us
  transfers between devices with their start and end apart: 17, of which 7 were waited for; matrix products, arithmetic and copies ran while one was open for 9% of the time, Pallas kernels for 0%

commit v1 on v0

v1 whole, which is shorter than its diff:
```python
import functools

import jax
import jax.numpy as jnp
from jax import lax
from jax.experimental import pallas as pl
from jax.experimental.pallas import tpu as pltpu
from jax.sharding import PartitionSpec as P

HD = 128
GROUP = 2
W = 1024
REACH = 4

attn_scale = 168.0 ** (-0.5)
LOG2E = 1.4426950408889634
NEG = -1e30
MESH = pl.DeviceIdType.MESH
F32 = jnp.float32
BF16 = jnp.bfloat16


def dot_nt(a, b):
    return lax.dot_general(a, b, (((1,), (1,)), ((), ())), preferred_element_type=F32)


def dot_nn(a, b):
    return lax.dot_general(a, b, (((1,), (0,)), ((), ())), preferred_element_type=F32)


def dot_tn(a, b):
    return lax.dot_general(a, b, (((0,), (0,)), ((), ())), preferred_element_type=F32)


def attention(
    n,
    nh,
    rows,
    q_ref,
    k_ref,
    v_ref,
    g_ref,
    dq_ref,
    dk_ref,
    dv_ref,
    buf,
    qp,
    gp,
    acc,
    sb,
    rv,
    s_sc,
    send_f,
    recv_f,
    send_r,
    recv_r,
):
    c = lax.axis_index("ctx")
    x = lax.rem(c, 2)
    even = x == 0
    odd = x == 1
    pair = c + 1 - 2 * x
    up = c + 2 < n
    down = c >= 2

    barrier = pltpu.get_barrier_semaphore()

    def greet(target):
        pl.semaphore_signal(barrier, inc=1, device_id={"ctx": target}, device_id_type=MESH)

    greet(pair)
    pl.when(up)(lambda: greet(c + 2))
    pl.when(down)(lambda: greet(c - 2))

    def cols(h, width):
        return pl.ds(pl.multiple_of(h * width, width), width)

    def pack(h, carry):
        buf[0, h, 0] = k_ref[:, cols(h, HD)]
        buf[0, h, 1] = v_ref[:, cols(h, HD)]
        return carry

    lax.fori_loop(0, nh, pack, 0)

    pl.semaphore_wait(barrier, 1 + up.astype(jnp.int32) + down.astype(jnp.int32))

    def halo(src, dst, h, target):
        return pltpu.make_async_remote_copy(
            src_ref=buf.at[src, h],
            dst_ref=buf.at[dst, h],
            send_sem=send_f.at[dst - 1, h],
            recv_sem=recv_f.at[dst - 1, h],
            device_id={"ctx": target},
            device_id_type=MESH,
        )

    def back(d, h, target):
        return pltpu.make_async_remote_copy(
            src_ref=sb.at[d - 1, h],
            dst_ref=rv.at[d - 1, h],
            send_sem=send_r.at[d - 1, h],
            recv_sem=recv_r.at[d - 1, h],
            device_id={"ctx": target},
            device_id_type=MESH,
        )

    def send_own(h):
        pl.when(up)(lambda: halo(0, 2, h, c + 2).start())
        pl.when(even)(lambda: halo(0, 1, h, c + 1).start())

    send_own(0)
    send_own(1)

    def pack_q(h, carry):
        for i in range(GROUP):
            qp[h, i * rows : (i + 1) * rows] = q_ref[:, cols(h * GROUP + i, HD)]
            gp[h, i * rows : (i + 1) * rows] = g_ref[:, cols(h * GROUP + i, HD)]
        return carry

    lax.fori_loop(0, nh, pack_q, 0)

    for d in range(1, REACH + 1):

        @pl.when(c < d)
        def _():
            buf[d] = jnp.zeros(buf.shape[1:], BF16)

    def forward(h):
        @pl.when(down)
        def _():
            halo(0, 2, h, pair).wait_recv()

            @pl.when(up)
            def _():
                halo(2, 4, h, c + 2).start()

            @pl.when(even)
            def _():
                halo(2, 3, h, pair).start()

            @pl.when(odd)
            def _():
                halo(2, 1, h, pair).start()

        @pl.when(h + 2 < nh)
        def _():
            send_own(h + 2)

        @pl.when(c >= 4)
        def _():
            halo(2, 4, h, pair).wait_recv()

            @pl.when(odd)
            def _():
                halo(4, 3, h, pair).start()

        pl.when(c >= 1)(lambda: halo(0, 1, h, pair).wait_recv())
        pl.when(c >= 3)(lambda: halo(0, 3, h, pair).wait_recv())

    wide = GROUP * rows
    key_at = lax.broadcasted_iota(jnp.int32, (rows, wide), 0)
    query_at = lax.rem(lax.broadcasted_iota(jnp.int32, (rows, wide), 1), rows)

    def compute(h):
        q = qp[h]
        g = gp[h]
        tri = key_at <= query_at
        factor = attn_scale * LOG2E
        far = jnp.where(c >= 4, 0.0, NEG)
        s0 = jnp.where(tri, dot_nt(buf[0, h, 0], q) * factor, dot_nt(buf[4, h, 0], q) * factor + far)
        s_sc[0] = s0
        top = jnp.max(s0, axis=0, keepdims=True)
        for d in range(1, REACH):
            s = dot_nt(buf[d, h, 0], q) * factor + jnp.where(c >= d, 0.0, NEG)
            s_sc[d] = s
            top = jnp.maximum(top, jnp.max(s, axis=0, keepdims=True))
        total = jnp.zeros((1, wide), F32)
        delta = jnp.zeros((1, wide), F32)
        for d in range(REACH):
            e = jnp.exp2(s_sc[d] - top)
            if d == 0:
                gpr = jnp.where(tri, dot_nt(buf[0, h, 1], g), dot_nt(buf[4, h, 1], g))
            else:
                gpr = dot_nt(buf[d, h, 1], g)
            total += jnp.sum(e, axis=0, keepdims=True)
            delta += jnp.sum(e * gpr, axis=0, keepdims=True)
            s_sc[d] = e
            s_sc[REACH + d] = gpr
        inv = 1.0 / total
        delta = delta * inv
        dq = jnp.zeros((HD, wide), F32)
        for d in range(REACH):
            p = s_sc[d] * inv
            ds = p * (s_sc[REACH + d] - delta)
            if d == 0:
                parts = (
                    (0, jnp.where(tri, p, 0.0), jnp.where(tri, ds, 0.0)),
                    (4, jnp.where(tri, 0.0, p), jnp.where(tri, 0.0, ds)),
                )
            else:
                parts = ((d, p, ds),)
            for slot, p_part, ds_part in parts:
                p_low = p_part.astype(BF16)
                ds_low = ds_part.astype(BF16)
                dk = attn_scale * dot_nn(ds_low, q)
                dv = dot_nn(p_low, g)
                dq += dot_tn(buf[slot, h, 0], ds_low)
                if slot % 2:
                    sb[slot - 1, h, 0] = dk.astype(BF16)
                    sb[slot - 1, h, 1] = dv.astype(BF16)
                else:
                    acc[slot // 2, h, 0] = dk
                    acc[slot // 2, h, 1] = dv
        dq = (dq * attn_scale).T.astype(BF16)
        for i in range(GROUP):
            dq_ref[:, cols(h * GROUP + i, HD)] = dq[i * rows : (i + 1) * rows]

        pl.when(c >= 1)(lambda: back(1, h, pair).start())
        pl.when(c >= 3)(lambda: back(3, h, pair).start())

    def add(slot, d, h):
        acc[slot, h] += rv[d - 1, h].astype(F32)

    def stage_b(h):
        @pl.when(pair >= 3)
        def _():
            back(3, h, pair).wait_recv()
            pl.when(odd)(lambda: add(2, 3, h))
            pl.when(even)(lambda: add(1, 3, h))

        @pl.when(c >= 4)
        def _():
            sb[3, h] = acc[2, h].astype(BF16)
            back(4, h, c - 2).start()

        @pl.when(pair >= 1)
        def _():
            back(1, h, pair).wait_recv()
            pl.when(odd)(lambda: add(1, 1, h))
            pl.when(even)(lambda: add(0, 1, h))

    def stage_c(h):
        @pl.when(down)
        def _():
            @pl.when(up)
            def _():
                back(4, h, pair).wait_recv()
                add(1, 4, h)

            sb[1, h] = acc[1, h].astype(BF16)
            back(2, h, c - 2).start()

    def stage_d(h):
        @pl.when(up)
        def _():
            back(2, h, pair).wait_recv()
            add(0, 2, h)

        dk_ref[:, cols(h, HD)] = acc[0, h, 0].astype(BF16)
        dv_ref[:, cols(h, HD)] = acc[0, h, 1].astype(BF16)

    def step(i, carry):
        @pl.when(i < nh)
        def _():
            forward(i)
            compute(i)

        @pl.when((i >= 1) & (i < nh + 1))
        def _():
            stage_b(i - 1)

        @pl.when((i >= 2) & (i < nh + 2))
        def _():
            stage_c(i - 2)

        @pl.when(i >= 3)
        def _():
            stage_d(i - 3)

        return carry

    lax.fori_loop(0, nh + 3, step, 0)

    def drain(h, carry):
        pl.when(up)(lambda: halo(0, 2, h, pair).wait_send())
        pl.when(even)(lambda: halo(0, 1, h, pair).wait_send())
        pl.when(down & up)(lambda: halo(2, 4, h, pair).wait_send())
        pl.when(down & even)(lambda: halo(2, 3, h, pair).wait_send())
        pl.when(down & odd)(lambda: halo(2, 1, h, pair).wait_send())
        pl.when((c >= 4) & odd)(lambda: halo(4, 3, h, pair).wait_send())
        pl.when(c >= 1)(lambda: back(1, h, pair).wait_send())
        pl.when(c >= 3)(lambda: back(3, h, pair).wait_send())
        pl.when(c >= 4)(lambda: back(4, h, pair).wait_send())
        pl.when(down)(lambda: back(2, h, pair).wait_send())
        return carry

    lax.fori_loop(0, nh, drain, 0)


def shards(n, normed_input, attn_queries, attn_keys, attn_values, out_grad):
    rows = attn_queries.shape[0]
    nh = attn_keys.shape[1] // HD
    assert rows * REACH == W and n % 2 == 0
    block = (2, rows, HD)
    vmem = pl.BlockSpec(memory_space=pltpu.VMEM)
    query_grad, key_low, value_low = pl.pallas_call(
        functools.partial(attention, n, nh, rows),
        out_shape=(
            jax.ShapeDtypeStruct(attn_queries.shape, BF16),
            jax.ShapeDtypeStruct(attn_keys.shape, BF16),
            jax.ShapeDtypeStruct(attn_keys.shape, BF16),
        ),
        in_specs=[vmem] * 4,
        out_specs=(vmem,) * 3,
        scratch_shapes=[
            pltpu.VMEM((REACH + 1, nh) + block, BF16),
            pltpu.VMEM((nh, GROUP * rows, HD), BF16),
            pltpu.VMEM((nh, GROUP * rows, HD), BF16),
            pltpu.VMEM((3, nh) + block, F32),
            pltpu.VMEM((REACH, nh) + block, BF16),
            pltpu.VMEM((REACH, nh) + block, BF16),
            pltpu.VMEM((2 * REACH, rows, GROUP * rows), F32),
            pltpu.SemaphoreType.DMA((REACH, nh)),
            pltpu.SemaphoreType.DMA((REACH, nh)),
            pltpu.SemaphoreType.DMA((REACH, nh)),
            pltpu.SemaphoreType.DMA((REACH, nh)),
        ],
        compiler_params=pltpu.CompilerParams(
            collective_id=0, has_side_effects=True, vmem_limit_bytes=48 * 1024 * 1024
        ),
    )(attn_queries, attn_keys, attn_values, out_grad)
    partial_term = dot_tn(normed_input, key_low)
    summed = lax.psum_scatter(partial_term, "ctx", scatter_dimension=0, tiled=True)
    return (query_grad, summed, value_low)


def solution(mesh):
    return jax.shard_map(
        functools.partial(shards, mesh.shape["ctx"]),
        mesh=mesh,
        in_specs=(
            P(("groups", "ctx"), None),
            P(("groups", "ctx"), "tp"),
            P(("groups", "ctx"), "tp"),
            P(("groups", "ctx"), "tp"),
            P(("groups", "ctx"), "tp"),
        ),
        out_specs=(
            P(("groups", "ctx"), "tp"),
            P(("groups", "ctx"), "tp"),
            P(("groups", "ctx"), "tp"),
        ),
        check_vma=False,
    )
```

time: 364 us -> 208 us (0.57)
  waiting for transfers between devices: 225 us -> 107 us
  Pallas kernels: 0 us -> 71.4 us
  starting transfers between devices: 45.5 us -> 0.04 us
  matrix products: 44.8 us -> 3.36 us
  local copies, waits for them, and re-layouts: 25.4 us -> 11.8 us
  other arithmetic: 7.22 us -> 0 us
    ppermute x16 -> x0, waiting for transfers between devices: 167 us -> none  [shifted(): lax.ppermute(value, axis, [(source, source + steps) for source in range(f...]
    pallas_call x0 -> x1, Pallas kernels: none -> 71.4 us  [shards(): pl.pallas_call(functools.partial(attention, n, nh, rows), out_shape=(jax....]
    unnamed x2, waiting for transfers between devices: 57.8 us -> 107 us
    ppermute x16 -> x0, starting transfers between devices: 45.5 us -> none  [shifted(): lax.ppermute(value, axis, [(source, source + steps) for source in range(f...]
    dot_general x17 -> x1, matrix products: 31.8 us -> 3.36 us  [dot_tn(): lax.dot_general(a, b, (((0,), (0,)), ((), ())), preferred_element_type=F32)]
    sub x4 -> x0, matrix products: 13 us -> none  [head_block(): raised = jnp.exp(scores - row_max)]
    unnamed x74 -> x13, local copies, waits for them, and re-layouts: 20.3 us -> 11.8 us
    slice x4 -> x0, local copies, waits for them, and re-layouts: 3.78 us -> none  [the longest x1 1.37 us: shards(): value_total[slot_index * edge_rows:(slot_index + 1) * edge_rows]]
  transfers between devices with their start and end apart: 17 -> 1, of which waited for: 7 -> 1; matrix products, arithmetic and copies ran while one was open for 9% -> 0% of each run, Pallas kernels for 0% -> 0%
where the time goes in v1:
time: 208 us; the launch traced here: 207 us
  waiting for transfers between devices  107 us (51%)
  Pallas kernels  71.4 us (34%)
  between operations  14.1 us (7%)
  local copies, waits for them, and re-layouts  11.8 us (6%)
  matrix products  3.36 us (2%)
    unnamed x2, waiting for transfers between devices  107 us
    pallas_call x1, Pallas kernels, shards(): pl.pallas_call(functools.partial(attention, n, nh, rows), out_shape=(jax....  71.4 us
    unnamed x13, local copies, waits for them, and re-layouts  11.8 us
  transfers between devices with their start and end apart: 1, of which 1 were waited for; matrix products, arithmetic and copies ran while one was open for 0% of the time, Pallas kernels for 0%

profile of v1, /device:TPU:0, one launch (start us, length us, event | category | flops | bytes accessed | tf_op | source)
XLA Modules:
  0.0 207.3 jit_solution(2747585394605063646)
XLA Ops:
  7.2 0.0 copy-start
  7.2 0.0 reduce-scatter.4.cloned.1.call-start
  7.2 0.0 copy-start.1
  7.2 1.1 copy-done.1
  8.4 0.0 copy-start.2
  8.4 1.0 copy-done.2
  9.4 0.0 copy-start.3
  9.4 0.9 copy-done.3
  10.4 0.0 copy-start.4
  10.4 0.9 copy-done.4
  11.3 71.4 %shard_map.76 = (bf16[256,1024]{1,0:T(8,128)(2,1)S(1)}, bf16[256,512]{1,0:T(8,128)(2,1)S(1)}, bf16[256,512]{1,0:T(8,128)(2,1)S(1)}) custom-call(bf16[256,1024]{1,0:T(8,128)(2,1)S(1)} %copy-done.1, bf16[256,512]{1,0:T(8,128)(2,1)S(1)} %copy-done.3, bf16[256,512]{1,0:T(8,128)(2,1)S(1)} %copy-done.4, bf16[256,1024]{1,0:T(8,128)(2,1)S(1)} %copy-done.2), custom_call_target="tpu_custom_call" | custom-call | tf_op jit(solution)/shard_map/pallas_call | solution.py:306
  82.7 0.0 copy-done
  82.7 3.4 %convolution_bitcast_fusion = f32[2688,512]{0,1:T(8,128)} fusion(bf16[256,512]{1,0:T(8,128)(2,1)S(1)} %get-tuple-element.7, bf16[256,2688]{1,0:T(8,128)(2,1)S(1)} %copy-done), kind=kOutput, calls=%fused_computation | convolution fusion | flops 704643072 | bytes 7143424 | tf_op jit(solution)/shard_map/dot_general | solution.py:32
  86.0 6.3 %copy.10 = f32[2688,512]{1,0:T(8,128)} copy(f32[2688,512]{0,1:T(8,128)} %convolution_bitcast_fusion) | data formatting | bytes 11010048
  92.3 0.0 reduce-scatter.4.cloned.1.call-update
  92.3 106.7 %reduce-scatter.4.cloned.1.call-done = f32[336,512]{1,0:T(8,128)} async-done(((f32[2688,512]{1,0:T(8,128)}), f32[336,512]{1,0:T(8,128)}) %reduce-scatter.4.cloned.1.call-update) | async-done | bytes 688144
  199.0 0.8 copy.14
  199.8 0.7 copy.15
Async XLA Ops:
  7.2 75.5 %copy-start = (bf16[256,2688]{1,0:T(8,128)(2,1)S(1)}, bf16[256,2688]{1,0:T(8,128)(2,1)}, u32[]{:S(2)}) copy-start(bf16[256,2688]{1,0:T(8,128)(2,1)} %param.5) | copy-start | bytes 4128772
  7.2 191.8 %reduce-scatter.4.cloned.1.call-start = ((), (), s32[]{:S(2)}) async-start(), calls=%async_computation.1 | async-start | bytes 6193152
  7.2 1.1 copy-start.1
  8.4 1.0 copy-start.2
  9.4 0.9 copy-start.3
  10.4 0.9 copy-start.4
Sparse Core Ops, SparseCore 0:
  92.5 106.4 reduce-scatter.3

commit v2 on v1

--- a/solution.py
+++ b/solution.py
@@ -36,10 +36,12 @@
     n,
     nh,
     rows,
+    fused,
     q_ref,
     k_ref,
     v_ref,
     g_ref,
+    x_ref,
     dq_ref,
     dk_ref,
     dv_ref,
@@ -54,6 +56,7 @@
     recv_f,
     send_r,
     recv_r,
+    *more,
 ):
     c = lax.axis_index("ctx")
     x = lax.rem(c, 2)
@@ -68,9 +71,23 @@
     def greet(target):
         pl.semaphore_signal(barrier, inc=1, device_id={"ctx": target}, device_id_type=MESH)
 
-    greet(pair)
-    pl.when(up)(lambda: greet(c + 2))
-    pl.when(down)(lambda: greet(c - 2))
+    if fused:
+        x_half, x_turned, x_got, x_all, gath, x_sem = more[:6]
+        send_x, recv_x, send_s, recv_s, send_p, recv_p, send_u, recv_u, send_d, recv_d = more[6:]
+        core = lax.axis_index("tp")
+        half = rows // 2
+        out_rows = x_all.shape[0]
+        load_x = pltpu.make_async_copy(
+            x_ref.at[pl.ds(pl.multiple_of(core * half, half), half)], x_half, x_sem
+        )
+        load_x.start()
+        for step in range(1, n):
+            greet(lax.rem(c + step, n))
+        pl.semaphore_signal(barrier, inc=1, device_id={"tp": 1 - core}, device_id_type=MESH)
+    else:
+        greet(pair)
+        pl.when(up)(lambda: greet(c + 2))
+        pl.when(down)(lambda: greet(c - 2))
 
     def cols(h, width):
         return pl.ds(pl.multiple_of(h * width, width), width)
@@ -82,7 +99,10 @@
 
     lax.fori_loop(0, nh, pack, 0)
 
-    pl.semaphore_wait(barrier, 1 + up.astype(jnp.int32) + down.astype(jnp.int32))
+    if fused:
+        pl.semaphore_wait(barrier, n)
+    else:
+        pl.semaphore_wait(barrier, 1 + up.astype(jnp.int32) + down.astype(jnp.int32))
 
     def halo(src, dst, h, target):
         return pltpu.make_async_remote_copy(
@@ -118,6 +138,110 @@
         return carry
 
     lax.fori_loop(0, nh, pack_q, 0)
+
+    if fused:
+        z = c // 2
+        nz = n // 2
+
+        def x_copy(src, target):
+            return pltpu.make_async_remote_copy(
+                src_ref=x_turned.at[pl.ds(pl.multiple_of(target * out_rows, 16), out_rows)],
+                dst_ref=x_got.at[src, core],
+                send_sem=send_x.at[target],
+                recv_sem=recv_x.at[src],
+                device_id={"ctx": target},
+                device_id_type=MESH,
+            )
+
+        def x_share(src, side):
+            return pltpu.make_async_remote_copy(
+                src_ref=x_got.at[src, side],
+                dst_ref=x_got.at[src, side],
+                send_sem=send_s.at[src],
+                recv_sem=recv_s.at[src],
+                device_id={"tp": 1 - core},
+                device_id_type=MESH,
+            )
+
+        def gather_pair(h, block):
+            return pltpu.make_async_remote_copy(
+                src_ref=gath.at[h, block],
+                dst_ref=gath.at[h, block],
+                send_sem=send_p.at[h],
+                recv_sem=recv_p.at[h],
+                device_id={"ctx": pair},
+                device_id_type=MESH,
+            )
+
+        def gather_line(h, level, target, send, recv):
+            blocks = gath.at[h, pl.ds(level * 2, 2)]
+            return pltpu.make_async_remote_copy(
+                src_ref=blocks,
+                dst_ref=blocks,
+                send_sem=send.at[level, h],
+                recv_sem=recv.at[level, h],
+                device_id={"ctx": target},
+                device_id_type=MESH,
+            )
+
+        def gather_up(h, level, target):
+            return gather_line(h, level, target, send_u, recv_u)
+
+        def gather_down(h, level, target):
+            return gather_line(h, level, target, send_d, recv_d)
+
+        load_x.wait()
+        for at in range(0, x_half.shape[1], HD):
+            x_turned[at : at + HD] = x_half[:, at : at + HD].T
+
+        def send_x_if(wanted):
+            def one(target, carry):
+                @pl.when(wanted(target))
+                def _():
+                    x_copy(c, target).start()
+
+                return carry
+
+            lax.fori_loop(0, n, one, 0)
+
+        send_x_if(lambda target: target < c)
+        x_got[c, core] = x_turned[pl.ds(pl.multiple_of(c * out_rows, 16), out_rows)]
+        x_share(c, core).start()
+
+        def share_x(src, carry):
+            @pl.when(src != c)
+            def _():
+                x_copy(src, lax.rem(c + 1, n)).wait_recv()
+                x_share(src, core).start()
+
+            return carry
+
+        def collect_x():
+            for src in range(n):
+                x_share(src, 1 - core).wait_recv()
+            for src in range(n):
+                for side in range(2):
+                    at = src * rows + side * half
+                    x_all[:, at : at + half] = x_got[src, side]
+
+        def gather_first(h):
+            gather_pair(h, pair).wait_recv()
+            pl.when(up)(lambda: gather_up(h, z, c + 2).start())
+            pl.when(down)(lambda: gather_down(h, z, c - 2).start())
+
+        def gather_hop(k, h):
+            @pl.when(z >= k)
+            def _():
+                gather_up(h, z - k, pair).wait_recv()
+                pl.when(up)(lambda: gather_up(h, z - k, c + 2).start())
+
+            @pl.when(z + k < nz)
+            def _():
+                gather_down(h, z + k, pair).wait_recv()
+                pl.when(down)(lambda: gather_down(h, z + k, c - 2).start())
+
+        def project(h):
+            dk_ref[:, cols(h, HD)] = dot_nn(x_all[...], gath[h].reshape(n * rows, HD))
 
     for d in range(1, REACH + 1):
 
@@ -256,13 +380,19 @@
             back(2, h, pair).wait_recv()
             add(0, 2, h)
 
-        dk_ref[:, cols(h, HD)] = acc[0, h, 0].astype(BF16)
+        if fused:
+            gath[h, c] = acc[0, h, 0].astype(BF16)
+            gather_pair(h, c).start()
+        else:
+            dk_ref[:, cols(h, HD)] = acc[0, h, 0].astype(BF16)
         dv_ref[:, cols(h, HD)] = acc[0, h, 1].astype(BF16)
 
     def step(i, carry):
         @pl.when(i < nh)
         def _():
             forward(i)
+            if fused:
+                pl.when(i == min(2, nh - 1))(lambda: send_x_if(lambda target: target > c))
             compute(i)
 
         @pl.when((i >= 1) & (i < nh + 1))
@@ -273,13 +403,36 @@
         def _():
             stage_c(i - 2)
 
-        @pl.when(i >= 3)
+        @pl.when((i >= 3) & (i < nh + 3))
         def _():
             stage_d(i - 3)
 
+        if fused:
+
+            @pl.when((i >= 4) & (i < nh + 4))
+            def _():
+                gather_first(i - 4)
+
+            for k in range(1, nz):
+
+                @pl.when((i >= 4 + k) & (i < nh + 4 + k))
+                def _():
+                    gather_hop(k, i - 4 - k)
+
+            @pl.when(i == nh + 1)
+            def _():
+                lax.fori_loop(0, n, share_x, 0)
+
+            pl.when(i == nh + 3)(collect_x)
+
+            @pl.when(i >= last)
+            def _():
+                project(i - last)
+
         return carry
 
-    lax.fori_loop(0, nh + 3, step, 0)
+    last = max(3 + n // 2, nh + 3) if fused else 3
+    lax.fori_loop(0, nh + last, step, 0)
 
     def drain(h, carry):
         pl.when(up)(lambda: halo(0, 2, h, pair).wait_send())
@@ -292,46 +445,73 @@
         pl.when(c >= 3)(lambda: back(3, h, pair).wait_send())
         pl.when(c >= 4)(lambda: back(4, h, pair).wait_send())
         pl.when(down)(lambda: back(2, h, pair).wait_send())
+        if fused:
+            gather_pair(h, c).wait_send()
+            for level in range(nz):
+                pl.when(up & (level <= z))(lambda: gather_up(h, level, pair).wait_send())
+                pl.when(down & (level >= z))(lambda: gather_down(h, level, pair).wait_send())
         return carry
 
     lax.fori_loop(0, nh, drain, 0)
+    if fused:
+
+        def drain_x(src, carry):
+            pl.when(src != c)(lambda: x_copy(c, src).wait_send())
+            x_share(src, core).wait_send()
+            return carry
+
+        lax.fori_loop(0, n, drain_x, 0)
 
 
 def shards(n, normed_input, attn_queries, attn_keys, attn_values, out_grad):
     rows = attn_queries.shape[0]
     nh = attn_keys.shape[1] // HD
+    width = normed_input.shape[1]
     assert rows * REACH == W and n % 2 == 0
+    fused = n <= 16 and width % n == 0 and (width // n) % 16 == 0 and width % HD == 0
     block = (2, rows, HD)
     vmem = pl.BlockSpec(memory_space=pltpu.VMEM)
-    query_grad, key_low, value_low = pl.pallas_call(
-        functools.partial(attention, n, nh, rows),
+    dma = pltpu.SemaphoreType.DMA
+    scratch = [
+        pltpu.VMEM((REACH + 1, nh) + block, BF16),
+        pltpu.VMEM((nh, GROUP * rows, HD), BF16),
+        pltpu.VMEM((nh, GROUP * rows, HD), BF16),
+        pltpu.VMEM((3, nh) + block, F32),
+        pltpu.VMEM((REACH, nh) + block, BF16),
+        pltpu.VMEM((REACH, nh) + block, BF16),
+        pltpu.VMEM((2 * REACH, rows, GROUP * rows), F32),
+    ] + [dma((REACH, nh))] * 4
+    if fused:
+        key_out = jax.ShapeDtypeStruct((width // n, attn_keys.shape[1]), F32)
+        scratch += [
+            pltpu.VMEM((rows // 2, width), BF16),
+            pltpu.VMEM((width, rows // 2), BF16),
+            pltpu.VMEM((n, 2, width // n, rows // 2), BF16),
+            pltpu.VMEM((width // n, n * rows), BF16),
+            pltpu.VMEM((nh, n, rows, HD), BF16),
+            dma,
+        ]
+        scratch += [dma((n,))] * 4 + [dma((nh,))] * 2 + [dma((n // 2, nh))] * 4
+    else:
+        key_out = jax.ShapeDtypeStruct(attn_keys.shape, BF16)
+    query_grad, key_result, value_low = pl.pallas_call(
+        functools.partial(attention, n, nh, rows, fused),
         out_shape=(
             jax.ShapeDtypeStruct(attn_queries.shape, BF16),
-            jax.ShapeDtypeStruct(attn_keys.shape, BF16),
+            key_out,
             jax.ShapeDtypeStruct(attn_keys.shape, BF16),
         ),
-        in_specs=[vmem] * 4,
+        in_specs=[vmem] * 4 + [pl.BlockSpec(memory_space=pl.ANY)],
         out_specs=(vmem,) * 3,
-        scratch_shapes=[
-            pltpu.VMEM((REACH + 1, nh) + block, BF16),
-            pltpu.VMEM((nh, GROUP * rows, HD), BF16),
-            pltpu.VMEM((nh, GROUP * rows, HD), BF16),
-            pltpu.VMEM((3, nh) + block, F32),
-            pltpu.VMEM((REACH, nh) + block, BF16),
-            pltpu.VMEM((REACH, nh) + block, BF16),
-            pltpu.VMEM((2 * REACH, rows, GROUP * rows), F32),
-            pltpu.SemaphoreType.DMA((REACH, nh)),
-            pltpu.SemaphoreType.DMA((REACH, nh)),
-            pltpu.SemaphoreType.DMA((REACH, nh)),
-            pltpu.SemaphoreType.DMA((REACH, nh)),
-        ],
+        scratch_shapes=scratch,
         compiler_params=pltpu.CompilerParams(
             collective_id=0, has_side_effects=True, vmem_limit_bytes=48 * 1024 * 1024
         ),
-    )(attn_queries, attn_keys, attn_values, out_grad)
-    partial_term = dot_tn(normed_input, key_low)
-    summed = lax.psum_scatter(partial_term, "ctx", scatter_dimension=0, tiled=True)
-    return (query_grad, summed, value_low)
+    )(attn_queries, attn_keys, attn_values, out_grad, normed_input)
+    if not fused:
+        partial_term = dot_tn(normed_input, key_result)
+        key_result = lax.psum_scatter(partial_term, "ctx", scatter_dimension=0, tiled=True)
+    return (query_grad, key_result, value_low)
 
 
 def solution(mesh):

time: 208 us -> 116 us (0.56)
  waiting for transfers between devices: 107 us -> 0 us
  Pallas kernels: 71.4 us -> 108 us
  between operations: 14.1 us -> 0.65 us
  local copies, waits for them, and re-layouts: 11.8 us -> 7.66 us
  matrix products: 3.36 us -> 0 us
    unnamed x2 -> x0, waiting for transfers between devices: 107 us -> none
    pallas_call x1, Pallas kernels: 71.4 us -> 108 us  [shards(): pl.pallas_call(functools.partial(attention, n, nh, rows, fused), out_shap...]
    unnamed x13, local copies, waits for them, and re-layouts: 11.8 us -> 7.66 us
    dot_general x1 -> x0, matrix products: 3.36 us -> none  [dot_tn(): lax.dot_general(a, b, (((0,), (0,)), ((), ())), preferred_element_type=F32)]
  transfers between devices with their start and end apart: 1 -> 0, of which waited for: 1 -> 0; matrix products, arithmetic and copies ran while one was open for 0% -> 0% of each run, Pallas kernels for 0% -> 0%
where the time goes in v2:
time: 116 us
  Pallas kernels  108 us (93%)
  local copies, waits for them, and re-layouts  7.66 us (7%)
    pallas_call x1, Pallas kernels, shards(): pl.pallas_call(functools.partial(attention, n, nh, rows, fused), out_shap...  108 us
    unnamed x13, local copies, waits for them, and re-layouts  7.66 us

profile of v2, /device:TPU:0, one launch (start us, length us, event | category | flops | bytes accessed | tf_op | source)
XLA Modules:
  0.0 115.9 jit_solution(3329221409802827280)
XLA Ops:
  0.6 0.0 copy-start
  0.6 1.3 %copy-done = bf16[256,2688]{1,0:T(8,128)(2,1)S(1)} copy-done((bf16[256,2688]{1,0:T(8,128)(2,1)S(1)}, bf16[256,2688]{1,0:T(8,128)(2,1)}, u32[]{:S(2)}) %copy-start) | copy-done | bytes 1376280
  2.0 0.0 copy-start.1
  2.0 1.0 copy-done.1
  3.0 0.0 copy-start.2
  3.0 1.0 copy-done.2
  4.1 0.0 copy-start.3
  4.1 0.9 copy-done.3
  5.0 0.0 copy-start.4
  5.0 0.9 copy-done.4
  6.0 107.5 %shard_map.76 = (bf16[256,1024]{1,0:T(8,128)(2,1)S(1)}, f32[336,512]{1,0:T(8,128)S(1)}, bf16[256,512]{1,0:T(8,128)(2,1)S(1)}) custom-call(bf16[256,1024]{1,0:T(8,128)(2,1)S(1)} %copy-done.1, bf16[256,512]{1,0:T(8,128)(2,1)S(1)} %copy-done.3, bf16[256,512]{1,0:T(8,128)(2,1)S(1)} %copy-done.4, bf16[256,1024]{1,0:T(8,128)(2,1)S(1)} %copy-done.2, ...), custom_call_target="tpu_custom_call" | custom-call | tf_op jit(solution)/shard_map/pallas_call | solution.py:497
  113.5 0.8 copy.11
  114.3 0.8 copy.12
  115.2 0.7 copy.13
Async XLA Ops:
  0.6 1.3 %copy-start = (bf16[256,2688]{1,0:T(8,128)(2,1)S(1)}, bf16[256,2688]{1,0:T(8,128)(2,1)}, u32[]{:S(2)}) copy-start(bf16[256,2688]{1,0:T(8,128)(2,1)} %x_ref.1) | copy-start | bytes 4128772
  2.0 1.0 copy-start.1
  3.0 1.0 copy-start.2
  4.1 0.9 copy-start.3
  5.0 0.9 copy-start.4

commit v3 on v2

--- a/solution.py
+++ b/solution.py
@@ -72,11 +72,12 @@
         pl.semaphore_signal(barrier, inc=1, device_id={"ctx": target}, device_id_type=MESH)
 
     if fused:
-        x_half, x_turned, x_got, x_all, gath, x_sem = more[:6]
-        send_x, recv_x, send_s, recv_s, send_p, recv_p, send_u, recv_u, send_d, recv_d = more[6:]
+        x_half, x_turned, x_got, x_all, gath, give, take, x_sem = more[:8]
+        send_x, recv_x, send_s, recv_s, send_p, recv_p, send_u, recv_u, send_d, recv_d = more[8:]
         core = lax.axis_index("tp")
         half = rows // 2
         out_rows = x_all.shape[0]
+        own_rows = out_rows // 2
         load_x = pltpu.make_async_copy(
             x_ref.at[pl.ds(pl.multiple_of(core * half, half), half)], x_half, x_sem
         )
@@ -149,7 +150,7 @@
                 dst_ref=x_got.at[src, core],
                 send_sem=send_x.at[target],
                 recv_sem=recv_x.at[src],
-                device_id={"ctx": target},
+                device_id={"ctx": target * 2 + x},
                 device_id_type=MESH,
             )
 
@@ -163,10 +164,10 @@
                 device_id_type=MESH,
             )
 
-        def gather_pair(h, block):
+        def trade(h):
             return pltpu.make_async_remote_copy(
-                src_ref=gath.at[h, block],
-                dst_ref=gath.at[h, block],
+                src_ref=give.at[h],
+                dst_ref=take.at[h],
                 send_sem=send_p.at[h],
                 recv_sem=recv_p.at[h],
                 device_id={"ctx": pair},
@@ -174,7 +175,7 @@
             )
 
         def gather_line(h, level, target, send, recv):
-            blocks = gath.at[h, pl.ds(level * 2, 2)]
+            blocks = gath.at[h, level]
             return pltpu.make_async_remote_copy(
                 src_ref=blocks,
                 dst_ref=blocks,
@@ -198,34 +199,33 @@
             def one(target, carry):
                 @pl.when(wanted(target))
                 def _():
-                    x_copy(c, target).start()
+                    x_copy(z, target).start()
 
                 return carry
 
-            lax.fori_loop(0, n, one, 0)
-
-        send_x_if(lambda target: target < c)
-        x_got[c, core] = x_turned[pl.ds(pl.multiple_of(c * out_rows, 16), out_rows)]
-        x_share(c, core).start()
+            lax.fori_loop(0, nz, one, 0)
+
+        send_x_if(lambda target: target < z)
+        x_got[z, core] = x_turned[pl.ds(pl.multiple_of(z * out_rows, 16), out_rows)]
+        x_share(z, core).start()
 
         def share_x(src, carry):
-            @pl.when(src != c)
-            def _():
-                x_copy(src, lax.rem(c + 1, n)).wait_recv()
+            @pl.when(src != z)
+            def _():
+                x_copy(src, lax.rem(z + 1, nz)).wait_recv()
                 x_share(src, core).start()
 
             return carry
 
         def collect_x():
-            for src in range(n):
+            for src in range(nz):
                 x_share(src, 1 - core).wait_recv()
-            for src in range(n):
+            for src in range(nz):
                 for side in range(2):
                     at = src * rows + side * half
                     x_all[:, at : at + half] = x_got[src, side]
 
         def gather_first(h):
-            gather_pair(h, pair).wait_recv()
             pl.when(up)(lambda: gather_up(h, z, c + 2).start())
             pl.when(down)(lambda: gather_down(h, z, c - 2).start())
 
@@ -241,7 +241,18 @@
                 pl.when(down)(lambda: gather_down(h, z + k, c - 2).start())
 
         def project(h):
-            dk_ref[:, cols(h, HD)] = dot_nn(x_all[...], gath[h].reshape(n * rows, HD))
+            blocks = gath[h].reshape(nz * rows, HD)
+
+            def part(side):
+                return dot_nn(x_all[pl.ds(pl.multiple_of(side * own_rows, 16), own_rows)], blocks)
+
+            give[h] = part(1 - x).astype(BF16)
+            trade(h).start()
+            dk_ref[:, cols(h, HD)] = part(x)
+
+        def finish(h):
+            trade(h).wait_recv()
+            dk_ref[:, cols(h, HD)] += take[h].astype(F32)
 
     for d in range(1, REACH + 1):
 
@@ -270,6 +281,7 @@
         def _():
             send_own(h + 2)
 
+    def forward_far(h):
         @pl.when(c >= 4)
         def _():
             halo(2, 4, h, pair).wait_recv()
@@ -278,6 +290,7 @@
             def _():
                 halo(4, 3, h, pair).start()
 
+    def arrived(h):
         pl.when(c >= 1)(lambda: halo(0, 1, h, pair).wait_recv())
         pl.when(c >= 3)(lambda: halo(0, 3, h, pair).wait_recv())
 
@@ -381,58 +394,40 @@
             add(0, 2, h)
 
         if fused:
-            gath[h, c] = acc[0, h, 0].astype(BF16)
-            gather_pair(h, c).start()
+            gath[h, z] = acc[0, h, 0].astype(BF16)
+            gather_first(h)
         else:
             dk_ref[:, cols(h, HD)] = acc[0, h, 0].astype(BF16)
         dv_ref[:, cols(h, HD)] = acc[0, h, 1].astype(BF16)
 
+    def stage(i, lag, run):
+        pl.when((i >= lag) & (i < nh + lag))(lambda: run(i - lag))
+
     def step(i, carry):
-        @pl.when(i < nh)
-        def _():
-            forward(i)
-            if fused:
-                pl.when(i == min(2, nh - 1))(lambda: send_x_if(lambda target: target > c))
-            compute(i)
-
-        @pl.when((i >= 1) & (i < nh + 1))
-        def _():
-            stage_b(i - 1)
-
-        @pl.when((i >= 2) & (i < nh + 2))
-        def _():
-            stage_c(i - 2)
-
-        @pl.when((i >= 3) & (i < nh + 3))
-        def _():
-            stage_d(i - 3)
-
+        stage(i, 0, forward)
+        stage(i, 1, forward_far)
         if fused:
-
-            @pl.when((i >= 4) & (i < nh + 4))
-            def _():
-                gather_first(i - 4)
-
+            pl.when(i == nh)(lambda: send_x_if(lambda target: target > z))
+        stage(i, 2, arrived)
+        stage(i, 2, compute)
+        stage(i, 3, stage_b)
+        stage(i, 4, stage_c)
+        stage(i, 5, stage_d)
+        if fused:
             for k in range(1, nz):
-
-                @pl.when((i >= 4 + k) & (i < nh + 4 + k))
-                def _():
-                    gather_hop(k, i - 4 - k)
-
-            @pl.when(i == nh + 1)
-            def _():
-                lax.fori_loop(0, n, share_x, 0)
-
-            pl.when(i == nh + 3)(collect_x)
-
-            @pl.when(i >= last)
-            def _():
-                project(i - last)
-
+                stage(i, 5 + k, functools.partial(gather_hop, k))
+
+            @pl.when(i == nh + 4)
+            def _():
+                lax.fori_loop(0, nz, share_x, 0)
+
+            pl.when(i == last)(collect_x)
+            stage(i, last, project)
+            stage(i, last + 1, finish)
         return carry
 
-    last = max(3 + n // 2, nh + 3) if fused else 3
-    lax.fori_loop(0, nh + last, step, 0)
+    last = max(4 + n // 2, nh + 5) if fused else 5
+    lax.fori_loop(0, nh + last + (1 if fused else 0), step, 0)
 
     def drain(h, carry):
         pl.when(up)(lambda: halo(0, 2, h, pair).wait_send())
@@ -446,7 +441,7 @@
         pl.when(c >= 4)(lambda: back(4, h, pair).wait_send())
         pl.when(down)(lambda: back(2, h, pair).wait_send())
         if fused:
-            gather_pair(h, c).wait_send()
+            trade(h).wait_send()
             for level in range(nz):
                 pl.when(up & (level <= z))(lambda: gather_up(h, level, pair).wait_send())
                 pl.when(down & (level >= z))(lambda: gather_down(h, level, pair).wait_send())
@@ -456,11 +451,11 @@
     if fused:
 
         def drain_x(src, carry):
-            pl.when(src != c)(lambda: x_copy(c, src).wait_send())
+            pl.when(src != z)(lambda: x_copy(z, src).wait_send())
             x_share(src, core).wait_send()
             return carry
 
-        lax.fori_loop(0, n, drain_x, 0)
+        lax.fori_loop(0, nz, drain_x, 0)
 
 
 def shards(n, normed_input, attn_queries, attn_keys, attn_values, out_grad):
@@ -486,12 +481,14 @@
         scratch += [
             pltpu.VMEM((rows // 2, width), BF16),
             pltpu.VMEM((width, rows // 2), BF16),
-            pltpu.VMEM((n, 2, width // n, rows // 2), BF16),
-            pltpu.VMEM((width // n, n * rows), BF16),
-            pltpu.VMEM((nh, n, rows, HD), BF16),
+            pltpu.VMEM((n // 2, 2, 2 * width // n, rows // 2), BF16),
+            pltpu.VMEM((2 * width // n, n // 2 * rows), BF16),
+            pltpu.VMEM((nh, n // 2, rows, HD), BF16),
+            pltpu.VMEM((nh, width // n, HD), BF16),
+            pltpu.VMEM((nh, width // n, HD), BF16),
             dma,
         ]
-        scratch += [dma((n,))] * 4 + [dma((nh,))] * 2 + [dma((n // 2, nh))] * 4
+        scratch += [dma((n // 2,))] * 4 + [dma((nh,))] * 2 + [dma((n // 2, nh))] * 4
     else:
         key_out = jax.ShapeDtypeStruct(attn_keys.shape, BF16)
     query_grad, key_result, value_low = pl.pallas_call(

time: 116 us -> 100 us (0.86)
  Pallas kernels: 108 us -> 91.7 us
    pallas_call x1, Pallas kernels: 108 us -> 91.7 us  [shards(): pl.pallas_call(functools.partial(attention, n, nh, rows, fused), out_shap...]
where the time goes in v3:
time: 100 us
  Pallas kernels  91.7 us (92%)
  local copies, waits for them, and re-layouts  7.66 us (8%)
    pallas_call x1, Pallas kernels, shards(): pl.pallas_call(functools.partial(attention, n, nh, rows, fused), out_shap...  91.7 us
    unnamed x13, local copies, waits for them, and re-layouts  7.66 us

profile of v3, /device:TPU:0, one launch (start us, length us, event | category | flops | bytes accessed | tf_op | source)
XLA Modules:
  0.0 100.0 jit_solution(10991024161673095470)
XLA Ops:
  0.6 0.0 copy-start
  0.6 1.3 %copy-done = bf16[256,2688]{1,0:T(8,128)(2,1)S(1)} copy-done((bf16[256,2688]{1,0:T(8,128)(2,1)S(1)}, bf16[256,2688]{1,0:T(8,128)(2,1)}, u32[]{:S(2)}) %copy-start) | copy-done | bytes 1376280
  2.0 0.0 copy-start.1
  2.0 1.0 %copy-done.1 = bf16[256,1024]{1,0:T(8,128)(2,1)S(1)} copy-done((bf16[256,1024]{1,0:T(8,128)(2,1)S(1)}, bf16[256,1024]{1,0:T(8,128)(2,1)}, u32[]{:S(2)}) %copy-start.1) | copy-done | bytes 524312
  3.0 0.0 copy-start.2
  3.0 1.0 %copy-done.2 = bf16[256,1024]{1,0:T(8,128)(2,1)S(1)} copy-done((bf16[256,1024]{1,0:T(8,128)(2,1)S(1)}, bf16[256,1024]{1,0:T(8,128)(2,1)}, u32[]{:S(2)}) %copy-start.2) | copy-done | bytes 524312
  4.1 0.0 copy-start.3
  4.1 0.9 copy-done.3
  5.0 0.0 copy-start.4
  5.0 0.9 copy-done.4
  6.0 91.7 %shard_map.76 = (bf16[256,1024]{1,0:T(8,128)(2,1)S(1)}, f32[336,512]{1,0:T(8,128)S(1)}, bf16[256,512]{1,0:T(8,128)(2,1)S(1)}) custom-call(bf16[256,1024]{1,0:T(8,128)(2,1)S(1)} %copy-done.1, bf16[256,512]{1,0:T(8,128)(2,1)S(1)} %copy-done.3, bf16[256,512]{1,0:T(8,128)(2,1)S(1)} %copy-done.4, bf16[256,1024]{1,0:T(8,128)(2,1)S(1)} %copy-done.2, ...), custom_call_target="tpu_custom_call" | custom-call | tf_op jit(solution)/shard_map/pallas_call | solution.py:494
  97.6 0.8 copy.11
  98.4 0.8 copy.12
  99.3 0.7 copy.13
Async XLA Ops:
  0.6 1.3 %copy-start = (bf16[256,2688]{1,0:T(8,128)(2,1)S(1)}, bf16[256,2688]{1,0:T(8,128)(2,1)}, u32[]{:S(2)}) copy-start(bf16[256,2688]{1,0:T(8,128)(2,1)} %x_ref.1) | copy-start | bytes 4128772
  2.0 1.0 %copy-start.1 = (bf16[256,1024]{1,0:T(8,128)(2,1)S(1)}, bf16[256,1024]{1,0:T(8,128)(2,1)}, u32[]{:S(2)}) copy-start(bf16[256,1024]{1,0:T(8,128)(2,1)} %q_ref.1) | copy-start | bytes 1572868
  3.0 1.0 %copy-start.2 = (bf16[256,1024]{1,0:T(8,128)(2,1)S(1)}, bf16[256,1024]{1,0:T(8,128)(2,1)}, u32[]{:S(2)}) copy-start(bf16[256,1024]{1,0:T(8,128)(2,1)} %g_ref.1) | copy-start | bytes 1572868
  4.1 0.9 copy-start.3
  5.0 0.9 copy-start.4
